TPU v7x, 32 devices: a whole 2x2x4 slice. The times are simulated.
32 devices in a mesh: groups: 2 (over x), ep: 16 (over z, y, core).
Axes of the slice: x: 2, y: 2, z: 4, core: 2. Of those that a mesh axis runs over, the one named last changes fastest.
Arguments:
- residual: bfloat16 [128, 7168], P(('groups', 'ep')), parts along dimension 0, may hold values from -6 to 6
- queries: bfloat16 [128, 128, 192], P('groups', 'ep'), parts along dimension 0, may hold values from -60 to 60
- new_kv: bfloat16 [128, 576], P(('groups', 'ep')), parts along dimension 0, may hold values from -6 to 6
- kv_cache: bfloat16 [64, 384, 576], P(('groups', 'ep')), parts along dimension 0, may hold values from -9 to 9
- lengths: int32 [64], P(('groups', 'ep')), parts along dimension 0, may hold values from 2 to 384, as said below
- w_uk: bfloat16 [128, 128, 512], P('ep'), may hold values from -0.5 to 0.5
- w_uv: bfloat16 [128, 512, 128], P('ep'), may hold values from -0.75 to 0.75
- w_out: bfloat16 [16384, 7168], P('ep'), may hold values from -0.09375 to 0.09375
- norm_gain: float32 [7168], replicated, may hold values from 0.5 to 1.5
- w_gate: bfloat16 [7168, 8192], P(None, 'ep'), may hold values from -0.0625 to 0.0625
- w_up: bfloat16 [7168, 8192], P(None, 'ep'), may hold values from -0.0625 to 0.0625
- w_down: bfloat16 [8192, 7168], P('ep'), may hold values from -0.375 to 0.375
- route_ids: int32 [128, 2], P(('groups', 'ep')), parts along dimension 0, may hold values from 0 to 7, all different within a row; in each aligned block of 4 rows (0 to 3, 4 to 7, ...) at most 2 rows name the same one
- route_gates: float32 [128, 2], P(('groups', 'ep')), parts along dimension 0, may hold values from 0.2 to 1
Outputs:
- attn_out: bfloat16 [128, 7168], P(('groups', 'ep')), parts along dimension 0
- moe_out: bfloat16 [128, 7168], P(('groups', 'ep')), parts along dimension 0
There are 2 independent parts, one for each index of `groups`. A program takes and returns all parts, laid end to end along the dimension named above; an argument that names none is the same for every part. Nothing has to cross between parts.
Inputs may be any that keep to these rules, and one draw needn't show every extreme that they name: `lengths`: at least 2 valid slots; on every device some request uses all 384 slots. `route_ids`: each row names 2 different experts; among the rows of one device no expert is named more than 2 times.
All inputs are finite; a program needn't handle non-finite values.
Results may differ from a plain program's by a relative error of at most 0.013.
Values may be sent and summed in bfloat16 or wider, within the bound.
A program may use at most 128 MiB of HBM per device.

v0:
```python
import jax
import jax.numpy as jnp
from jax import lax
from jax.sharding import PartitionSpec as P

EXPERTS = 8


def latent_attention(q_home, new_kv, kv_cache, lengths, scale, lat_width):
    req_dev, seq_len, width = kv_cache.shape
    tok_dev, heads, _ = q_home.shape
    q_req = q_home.reshape(req_dev, 2 * heads, width)
    keys = jnp.concatenate([kv_cache, new_kv.reshape(req_dev, 2, width)], axis=1)
    scores = jnp.einsum("rqc,rkc->rqk", q_req, keys, preferred_element_type=jnp.float32) * scale
    position = jnp.arange(seq_len + 2)
    draft = jnp.arange(2 * heads) // heads
    valid = jnp.where(
        position[None, None, :] < seq_len,
        position[None, None, :] < lengths[:, None, None],
        (position - seq_len)[None, None, :] <= draft[None, :, None],
    )
    scores = jnp.where(valid, scores, -1e30)
    highest = jnp.max(scores, axis=-1, keepdims=True)
    powers = jnp.where(valid, jnp.exp(scores - highest), 0.0)
    probs = (powers / jnp.sum(powers, axis=-1, keepdims=True)).astype(jnp.bfloat16)
    latent = jnp.einsum(
        "rqk,rkc->rqc", probs, keys[:, :, :lat_width], preferred_element_type=jnp.float32
    )
    return latent.astype(jnp.bfloat16).reshape(tok_dev, heads, lat_width)


def slot_table(flat_ids, experts):
    onehot = (flat_ids[..., None] == jnp.arange(experts, dtype=jnp.int32)).astype(jnp.int32)
    ranked = jnp.cumsum(onehot, axis=-2) - onehot
    return jnp.sum(ranked * onehot, axis=-1)


def shards(
    residual,
    queries,
    new_kv,
    kv_cache,
    lengths,
    w_uk,
    w_uv,
    w_out,
    norm_gain,
    w_gate,
    w_up,
    w_down,
    route_ids,
    route_gates,
):
    dev_count = lax.axis_size("ep")
    nope = w_uk.shape[1]
    lat_width = w_uk.shape[2]
    tok_dev, model = residual.shape
    topk = route_ids.shape[1]
    pairs = tok_dev * topk
    capacity = tok_dev // 2
    split = dev_count // EXPERTS
    scale = queries.shape[2] ** (-0.5)
    q_lat = jnp.einsum(
        "thn,hnc->thc", queries[:, :, :nope], w_uk, preferred_element_type=jnp.float32
    ).astype(jnp.bfloat16)
    q_abs = jnp.concatenate([q_lat, queries[:, :, nope:]], axis=-1)
    q_home = lax.all_to_all(q_abs, "ep", split_axis=0, concat_axis=1, tiled=True)
    latent = latent_attention(q_home, new_kv, kv_cache, lengths, scale, lat_width)
    latent_heads = lax.all_to_all(latent, "ep", split_axis=1, concat_axis=0, tiled=True)
    v_out = jnp.einsum(
        "thc,hcv->thv", latent_heads, w_uv, preferred_element_type=jnp.float32
    ).astype(jnp.bfloat16)
    v_flat = v_out.reshape(v_out.shape[0], v_out.shape[1] * v_out.shape[2])
    attn = lax.psum_scatter(
        jnp.dot(v_flat, w_out, preferred_element_type=jnp.float32),
        "ep",
        scatter_dimension=0,
        tiled=True,
    )
    stream = residual.astype(jnp.float32) + attn
    normed = (
        stream * lax.rsqrt(jnp.mean(stream * stream, axis=-1, keepdims=True) + 1e-06) * norm_gain
    ).astype(jnp.bfloat16)
    token_map = jnp.arange(pairs)[:, None] // topk == jnp.arange(tok_dev)[None, :]
    own_ids = route_ids.reshape(pairs)
    own_slots = slot_table(own_ids, EXPERTS)
    own_chosen = (own_ids[None, None, :] == jnp.arange(EXPERTS)[:, None, None]) & (
        own_slots[None, None, :] == jnp.arange(capacity)[None, :, None]
    )
    rows_every = lax.all_gather(normed, "ep", axis=0, tiled=True)
    ids_every = lax.all_gather(route_ids, "ep", axis=0, tiled=True)
    my_expert = lax.axis_index("ep") // split
    ids_flat = ids_every.reshape(dev_count, pairs)
    slots = slot_table(ids_flat, EXPERTS)
    chosen = (ids_flat[:, None, :] == my_expert) & (
        slots[:, None, :] == jnp.arange(capacity)[None, :, None]
    )
    picker = jnp.einsum(
        "scq,qt->sct",
        chosen.astype(jnp.bfloat16),
        token_map.astype(jnp.bfloat16),
        preferred_element_type=jnp.float32,
    ).astype(jnp.bfloat16)
    gathered_rows = jnp.einsum(
        "sct,std->scd",
        picker,
        rows_every.reshape(dev_count, tok_dev, model),
        preferred_element_type=jnp.float32,
    ).astype(jnp.bfloat16)
    stacked = gathered_rows.reshape(-1, model)
    gate = jnp.dot(stacked, w_gate, preferred_element_type=jnp.float32)
    upward = jnp.dot(stacked, w_up, preferred_element_type=jnp.float32)
    act = (jax.nn.silu(gate) * upward).astype(jnp.bfloat16)
    partial_value = (
        jnp.dot(act, w_down, preferred_element_type=jnp.float32)
        .astype(jnp.bfloat16)
        .reshape(gathered_rows.shape)
    )
    returned = lax.all_to_all(partial_value, "ep", split_axis=0, concat_axis=0, tiled=True)
    summed = jnp.sum(returned.reshape(EXPERTS, split, capacity, model).astype(jnp.float32), axis=1)
    weights = jnp.where(own_chosen, route_gates.reshape(1, 1, pairs), 0.0)
    mixing = jnp.einsum(
        "ecq,qt->tec", weights, token_map.astype(jnp.float32), precision=lax.Precision.HIGHEST
    )
    moe = jnp.einsum("tec,ecd->td", mixing, summed, precision=lax.Precision.HIGHEST)
    return (attn.astype(jnp.bfloat16), moe.astype(jnp.bfloat16))


def solution(mesh):
    return jax.shard_map(
        shards,
        mesh=mesh,
        in_specs=(
            P(("groups", "ep"), None),
            P("groups", "ep", None),
            P(("groups", "ep"), None),
            P(("groups", "ep"), None, None),
            P(("groups", "ep")),
            P("ep", None, None),
            P("ep", None, None),
            P("ep", None),
            P(),
            P(None, "ep"),
            P(None, "ep"),
            P("ep", None),
            P(("groups", "ep"), None),
            P(("groups", "ep"), None),
        ),
        out_specs=(P(("groups", "ep"), None), P(("groups", "ep"), None)),
        check_vma=False,
    )
```

profile of v0, /device:TPU:0, one launch (start us, length us, event | category | flops | bytes accessed | tf_op | source)
XLA Modules:
  0.0 240.8 jit_solution(10955924173012261769)
XLA Ops:
  7.2 0.0 copy-start
  7.2 0.0 copy-start.6
  7.2 1.0 slice.10
  8.2 0.9 slice.9
  9.1 0.0 copy-done
  9.2 0.3 fusion.6
  9.4 0.1 pad_maximum_fusion
  9.5 1.2 copy.54
  10.8 7.4 %all-to-all-start = ((bf16[64,8,576]{2,1,0:T(8,128)(2,1)}), bf16[64,8,576]{2,1,0:T(8,128)(2,1)S(1)}, u32[]{:S(2)}, u32[]{:S(2)}) async-start(bf16[64,8,576]{2,1,0:T(8,128)(2,1)} %copy.54), calls=%async_computation | async-start | bytes 1310720 | tf_op jit(solution)/shard_map/all_to_all | solution.py:67
  18.2 0.7 reshape.214
  18.9 2.2 copy.56
  21.1 0.0 copy-start.4
  21.1 0.0 copy-done.6
  21.1 0.1 iota_compare_fusion.5
  21.2 0.1 broadcast_compare_fusion
  21.3 13.4 %all-to-all-done = bf16[64,8,576]{2,1,0:T(8,128)(2,1)S(1)} async-done(((bf16[64,8,576]{2,1,0:T(8,128)(2,1)}), bf16[64,8,576]{2,1,0:T(8,128)(2,1)S(1)}, u32[]{:S(2)}, u32[]{:S(2)}) %all-to-all-start) | async-done | bytes 589856 | tf_op jit(solution)/shard_map/all_to_all | solution.py:67
  34.8 0.9 copy.55
  35.7 3.2 %fusion.52 = (f32[2,256]{1,0:T(2,128)S(1)}, f32[2,256,386]{1,2,0:T(8,128)}) fusion(pred[256,386]{0,1:T(8,128)(4,1)S(1)} %broadcast_compare_fusion, pred[2,386]{1,0:T(4,128)(4,1)S(1)} %iota_compare_fusion.5, pred[386]{0:T(512)(128)(4,1)S(1)} %iota_compare_fusion.7, bf16[2,256,576]{2,1,0:T(8,128)(2,1)} %bitcast.51, bf16[2,2,576]{2,1,0:T(2,128)(2,1)S(1)} %reshape.214, ...), kind=kOutput, calls=%fused_computation.88 | convolution fusion | flops 230834560 | bytes 2371718 | tf_op jit(solution)/shard_map/sub | solution.py:24
  38.9 1.9 convolution_convert_fusion.3
  40.8 1.2 copy.58
  42.0 4.8 %all-to-all-start.1 = ((bf16[4,128,512]{2,0,1:T(4,128)(2,1)}), bf16[4,128,512]{2,0,1:T(4,128)(2,1)S(1)}, u32[]{:S(2)}, u32[]{:S(2)}) async-start(bf16[4,128,512]{2,0,1:T(4,128)(2,1)} %copy.58), calls=%async_computation.1 | async-start | bytes 1048576 | tf_op jit(solution)/shard_map/all_to_all | solution.py:69
  46.8 0.0 all-reduce.3.cloned.1.call-start
  46.8 0.0 copy-done.4
  46.8 0.1 copy.61
  46.9 0.1 eq.110
  47.0 24.7 %all-gather = s32[16,4,2]{1,2,0:T(2,128)S(1)} all-gather(s32[1,4,2]{1,2,0:T(2,128)S(1)} %bitcast.55), channel_id=1, replica_groups=mesh['groups'=2,'ep'=16] {'ep'}, dimensions={0}, use_global_device_ids=true | all-gather | bytes 544 | tf_op jit(solution)/shard_map/all_gather | solution.py:91
  71.7 0.1 copy.63
  71.8 0.1 iota_compare_fusion.4
  71.9 0.0 all-to-all-done.1
  71.9 0.2 copy.79
  72.1 0.1 all_to_all.33
  72.2 0.0 copy-done.1
  72.2 0.3 fusion.7
  72.5 0.0 copy-start.5
  72.5 0.0 copy-start.7
  72.6 0.0 copy-start.2
  72.6 0.0 copy-start.3
  72.6 9.1 %fusion.18 = f32[64,7168]{1,0:T(8,128)} fusion(bf16[1024,7168]{1,0:T(8,128)(2,1)} %param.21, bf16[8,8,8,128]{3,2,1,0:T(8,128)(2,1)S(1)} %fusion.7), kind=kOutput, calls=%fused_computation.33 | convolution fusion | flops 939524096 | bytes 16646144 | tf_op jit(solution)/shard_map/dot_general | solution.py:75
  81.7 0.0 all-reduce.3.cloned.1.call-update
  81.7 0.0 copy-done.5
  81.7 0.1 copy.62
  81.8 0.1 broadcast_in_dim.68
  82.0 0.1 convolution_convert_fusion.5
  82.1 0.1 copy.64
  82.2 0.0 copy-done.7
  82.2 0.6 dynamic-slice
  83.4 0.2 select_reduce_fusion
  83.6 93.5 %all-reduce.3.cloned.1.call-done = f32[64,7168]{1,0:T(8,128)} async-done(((f32[64,7168]{1,0:T(8,128)}), f32[64,7168]{1,0:T(8,128)}) %all-reduce.3.cloned.1.call-update) | async-done | bytes 1835024
  177.2 0.0 copy-done.2
  177.2 1.1 multiply_reduce_fusion
  178.3 0.0 copy-done.3
  178.3 1.0 fusion.27
  179.3 22.1 %all-gather.1 = bf16[16,4,7168]{2,1,0:T(4,128)(2,1)S(1)} all-gather(bf16[1,4,7168]{2,1,0:T(4,128)(2,1)S(1)} %fusion.27), channel_id=1, replica_groups=mesh['groups'=2,'ep'=16] {'ep'}, dimensions={0}, use_global_device_ids=true | all-gather | bytes 974848 | tf_op jit(solution)/shard_map/all_gather | solution.py:90
  201.4 0.6 convolution_convert_fusion
  202.0 0.2 reshape.218
  202.2 4.4 %fusion.56 = f32[32,512]{1,0:T(8,128)S(1)} fusion(bf16[32,7168]{1,0:T(8,128)(2,1)S(1)} %reshape.218, bf16[7168,512]{1,0:T(8,128)(2,1)} %param.23), kind=kOutput, calls=%fused_computation.90 | convolution fusion | flops 234881024 | bytes 7864320 | tf_op jit(solution)/shard_map/dot_general | solution.py:111
  206.6 7.9 %convolution_convert_fusion.1 = bf16[32,7168]{1,0:T(8,128)(2,1)S(1)} fusion(bf16[512,7168]{1,0:T(8,128)(2,1)} %param.25, bf16[32,7168]{1,0:T(8,128)(2,1)S(1)} %reshape.218, bf16[7168,512]{1,0:T(8,128)(2,1)} %param.24, f32[32,512]{1,0:T(8,128)S(1)} %fusion.56), kind=kOutput, calls=%fused_computation.2 | convolution fusion | flops 470089728 | bytes 15663104 | tf_op jit(solution)/shard_map/dot_general | solution.py:115
  214.5 1.0 reshape.219
  215.5 3.6 %all-to-all-start.2 = ((bf16[16,2,7168]{2,1,0:T(2,128)(2,1)}), bf16[16,2,7168]{2,1,0:T(2,128)(2,1)S(1)}, u32[]{:S(2)}, u32[]{:S(2)}) async-start(bf16[16,2,7168]{2,1,0:T(2,128)(2,1)} %reshape.219), calls=%async_computation.2 | async-start | bytes 917504 | tf_op jit(solution)/shard_map/all_to_all | solution.py:119
  219.1 0.1 fusion.31
  219.2 1.7 dynamic-slice_convert_fusion
  220.8 11.4 %all-to-all-done.2 = bf16[16,2,7168]{2,1,0:T(2,128)(2,1)S(1)} async-done(((bf16[16,2,7168]{2,1,0:T(2,128)(2,1)}), bf16[16,2,7168]{2,1,0:T(2,128)(2,1)S(1)}, u32[]{:S(2)}, u32[]{:S(2)}) %all-to-all-start.2) | async-done | bytes 458784 | tf_op jit(solution)/shard_map/all_to_all | solution.py:119
  232.3 0.5 convert_reduce_fusion
  232.8 1.1 fusion.1
  (11 shorter events, 0.1 us)
Async XLA Ops:
  7.2 2.0 copy-start
  7.2 13.9 %copy-start.6 = (s32[2]{0:T(128)S(1)}, s32[2]{0:T(128)}, u32[]{:S(2)}) copy-start(s32[2]{0:T(128)} %param.18) | copy-start | bytes 28
  10.8 24.0 %all-to-all-start = ((bf16[64,8,576]{2,1,0:T(8,128)(2,1)}), bf16[64,8,576]{2,1,0:T(8,128)(2,1)S(1)}, u32[]{:S(2)}, u32[]{:S(2)}) async-start(bf16[64,8,576]{2,1,0:T(8,128)(2,1)} %copy.54), calls=%async_computation | async-start | bytes 1310720 | tf_op jit(solution)/shard_map/all_to_all | solution.py:67
  21.1 25.7 %copy-start.4 = (s32[4,2]{0,1:T(2,128)S(1)}, s32[4,2]{0,1:T(2,128)}, u32[]{:S(2)}) copy-start(s32[4,2]{0,1:T(2,128)} %param.26) | copy-start | bytes 100
  35.7 36.5 %copy-start.1 = (bf16[8,512,128]{2,1,0:T(8,128)(2,1)S(1)}, bf16[8,512,128]{2,1,0:T(8,128)(2,1)}, u32[]{:S(2)}) copy-start(bf16[8,512,128]{2,1,0:T(8,128)(2,1)} %param.20) | copy-start | bytes 3145732
  42.0 29.9 %all-to-all-start.1 = ((bf16[4,128,512]{2,0,1:T(4,128)(2,1)}), bf16[4,128,512]{2,0,1:T(4,128)(2,1)S(1)}, u32[]{:S(2)}, u32[]{:S(2)}) async-start(bf16[4,128,512]{2,0,1:T(4,128)(2,1)} %copy.58), calls=%async_computation.1 | async-start | bytes 1048576 | tf_op jit(solution)/shard_map/all_to_all | solution.py:69
  46.8 130.4 %all-reduce.3.cloned.1.call-start = ((), (), s32[]{:S(2)}) async-start(), calls=%async_computation.3 | async-start | bytes 3670016
  72.5 9.2 %copy-start.5 = (f32[4,2]{0,1:T(2,128)S(1)}, f32[4,2]{0,1:T(2,128)}, u32[]{:S(2)}) copy-start(f32[4,2]{0,1:T(2,128)} %param.27) | copy-start | bytes 100
  72.5 9.6 %copy-start.7 = (u32[32]{0:T(128)S(1)}, u32[32]{0:T(128)}, u32[]{:S(2)}) copy-start(u32[32]{0:T(128)} %constant.85) | copy-start | bytes 388
  72.6 104.6 %copy-start.2 = (bf16[4,7168]{1,0:T(4,128)(2,1)S(1)}, bf16[4,7168]{1,0:T(4,128)(2,1)}, u32[]{:S(2)}) copy-start(bf16[4,7168]{1,0:T(4,128)(2,1)} %param.14) | copy-start | bytes 172036
  72.6 105.7 %copy-start.3 = (f32[7168]{0:T(1024)S(1)}, f32[7168]{0:T(1024)}, u32[]{:S(2)}) copy-start(f32[7168]{0:T(1024)} %param.22) | copy-start | bytes 86020
  215.5 16.8 %all-to-all-start.2 = ((bf16[16,2,7168]{2,1,0:T(2,128)(2,1)}), bf16[16,2,7168]{2,1,0:T(2,128)(2,1)S(1)}, u32[]{:S(2)}, u32[]{:S(2)}) async-start(bf16[16,2,7168]{2,1,0:T(2,128)(2,1)} %reshape.219), calls=%async_computation.2 | async-start | bytes 917504 | tf_op jit(solution)/shard_map/all_to_all | solution.py:119
Sparse Core Ops, SparseCore 0:
  81.8 95.3 all-reduce.2
where the time goes:
time: 242 us; the launch traced here: 241 us
  waiting for transfers between devices  118 us (49%)
  blocking collectives  46.8 us (19%)
  matrix products  29.1 us (12%)
  starting transfers between devices  15.8 us (7%)
  between operations  14.9 us (6%)
  local copies, waits for them, and re-layouts  12.5 us (5%)
  other arithmetic  3.28 us (1%)
    unnamed x2, waiting for transfers between devices  93.6 us
    all_gather x1, blocking collectives, shards(): ids_every = lax.all_gather(route_ids, 'ep', axis=0, tiled=True)  24.7 us
    all_gather x1, blocking collectives, shards(): rows_every = lax.all_gather(normed, 'ep', axis=0, tiled=True)  22.1 us
    all_to_all x1, waiting for transfers between devices, shards(): lax.all_to_all(q_abs, 'ep', split_axis=0, concat_axis=1, tiled=True)  13.4 us
    all_to_all x1, waiting for transfers between devices, shards(): lax.all_to_all(partial_value, 'ep', split_axis=0, concat_axis=0, tiled=True)  11.4 us
    dot_general x1, matrix products, shards(): jnp.dot(v_flat, w_out, preferred_element_type=jnp.float32)  9.09 us
    dot_general x1, matrix products, shards(): jnp.dot(act, w_down, preferred_element_type=jnp.float32)  7.88 us
    all_to_all x1, starting transfers between devices, shards(): lax.all_to_all(q_abs, 'ep', split_axis=0, concat_axis=1, tiled=True)  7.39 us
  transfers between devices with their start and end apart: 4, of which 3 were waited for; matrix products, arithmetic and copies ran while one was open for 3% of the time, Pallas kernels for 0%

commit v1 on v0

v1 whole, which is shorter than its diff:
```python
import functools

import jax
import jax.numpy as jnp
from jax import lax
from jax.experimental import pallas as pl
from jax.experimental.pallas import tpu as pltpu
from jax.sharding import PartitionSpec as P

EXPERTS = 8


def latent_attention(q_home, new_kv, kv_cache, lengths, scale, lat_width):
    req_dev, seq_len, width = kv_cache.shape
    groups, rows, _ = q_home.shape
    part = rows // req_dev
    q_req = q_home.reshape(groups, req_dev, part, width)
    fresh = new_kv.reshape(req_dev, 2, width)
    old = jnp.einsum("grqc,rkc->rgqk", q_req, kv_cache, preferred_element_type=jnp.float32)
    new = jnp.einsum("grqc,rkc->rgqk", q_req, fresh, preferred_element_type=jnp.float32)
    draft = jnp.arange(part) // (part // 2)
    keep_old = (jnp.arange(seq_len) < lengths[:, None])[:, None, None, :]
    keep_new = (jnp.arange(2)[None, :] <= draft[:, None])[None, None]
    old = jnp.where(keep_old, old * scale, -1e30)
    new = jnp.where(keep_new, new * scale, -1e30)
    highest = jnp.maximum(
        jnp.max(old, axis=-1, keepdims=True), jnp.max(new, axis=-1, keepdims=True)
    )
    old = jnp.where(keep_old, jnp.exp(old - highest), 0.0)
    new = jnp.where(keep_new, jnp.exp(new - highest), 0.0)
    total = jnp.sum(old, axis=-1, keepdims=True) + jnp.sum(new, axis=-1, keepdims=True)
    old = (old / total).astype(jnp.bfloat16)
    new = (new / total).astype(jnp.bfloat16).astype(jnp.float32)
    latent = jnp.einsum(
        "rgqk,rkc->rgqc", old, kv_cache[:, :, :lat_width], preferred_element_type=jnp.float32
    )
    tail = fresh[:, None, None, :, :lat_width].astype(jnp.float32)
    latent = latent + new[..., 0:1] * tail[..., 0, :] + new[..., 1:2] * tail[..., 1, :]
    latent = latent.astype(jnp.bfloat16)
    return jnp.transpose(latent, (1, 0, 2, 3)).reshape(groups, rows, lat_width)


def exchange_kernel(n, share, in_ref, out_ref, send_sem, recv_sem, own_sem):
    me = lax.axis_index("ep")
    barrier = pltpu.get_barrier_semaphore()

    def greet(k, carry):
        pl.semaphore_signal(
            barrier,
            inc=1,
            device_id={"ep": lax.rem(me + k, n)},
            device_id_type=pl.DeviceIdType.MESH,
        )
        return carry

    lax.fori_loop(1, n, greet, 0)
    own = pltpu.make_async_copy(in_ref.at[me // share], out_ref.at[me], own_sem)
    own.start()
    pl.semaphore_wait(barrier, n - 1)

    def copy(k):
        target = lax.rem(me + k, n)
        return pltpu.make_async_remote_copy(
            src_ref=in_ref.at[target // share],
            dst_ref=out_ref.at[me],
            send_sem=send_sem.at[k],
            recv_sem=recv_sem.at[k],
            device_id={"ep": target},
            device_id_type=pl.DeviceIdType.MESH,
        )

    def start(k, carry):
        copy(k).start()
        return carry

    def finish(k, carry):
        copy(k).wait()
        return carry

    lax.fori_loop(1, n, start, 0)
    own.wait()
    lax.fori_loop(1, n, finish, 0)


def exchange(blocks, number, share=1):
    n = blocks.shape[0] * share
    shape = (n,) + blocks.shape[1:]
    return pl.pallas_call(
        functools.partial(exchange_kernel, n, share),
        out_shape=jax.ShapeDtypeStruct(shape, blocks.dtype),
        in_specs=[pl.BlockSpec(memory_space=pltpu.VMEM)],
        out_specs=pl.BlockSpec(memory_space=pltpu.VMEM),
        scratch_shapes=[
            pltpu.SemaphoreType.DMA((n,)),
            pltpu.SemaphoreType.DMA((n,)),
            pltpu.SemaphoreType.DMA,
        ],
        compiler_params=pltpu.CompilerParams(
            collective_id=number, has_side_effects=True, vmem_limit_bytes=32 * 2**20
        ),
    )(blocks)


def slot_table(flat_ids, experts):
    onehot = (flat_ids[..., None] == jnp.arange(experts, dtype=jnp.int32)).astype(jnp.int32)
    ranked = jnp.cumsum(onehot, axis=-2) - onehot
    return jnp.sum(ranked * onehot, axis=-1)


def shards(
    residual,
    queries,
    new_kv,
    kv_cache,
    lengths,
    w_uk,
    w_uv,
    w_out,
    norm_gain,
    w_gate,
    w_up,
    w_down,
    route_ids,
    route_gates,
):
    dev_count = lax.axis_size("ep")
    nope = w_uk.shape[1]
    lat_width = w_uk.shape[2]
    tok_dev, model = residual.shape
    topk = route_ids.shape[1]
    pairs = tok_dev * topk
    capacity = tok_dev // 2
    split = dev_count // EXPERTS
    scale = queries.shape[2] ** (-0.5)
    q_lat = jnp.einsum(
        "thn,hnc->thc", queries[:, :, :nope], w_uk, preferred_element_type=jnp.float32
    ).astype(jnp.bfloat16)
    q_abs = jnp.concatenate([q_lat, queries[:, :, nope:]], axis=-1)
    heads_dev = q_abs.shape[1]
    q_home = exchange(q_abs.reshape(dev_count, tok_dev * heads_dev, q_abs.shape[2]), 0)
    latent = latent_attention(q_home, new_kv, kv_cache, lengths, scale, lat_width)
    latent_heads = exchange(latent, 1).reshape(dev_count * tok_dev, heads_dev, lat_width)
    v_out = jnp.einsum(
        "thc,hcv->thv", latent_heads, w_uv, preferred_element_type=jnp.float32
    ).astype(jnp.bfloat16)
    v_flat = v_out.reshape(v_out.shape[0], v_out.shape[1] * v_out.shape[2])
    share = jnp.dot(v_flat, w_out, preferred_element_type=jnp.float32).astype(jnp.bfloat16)
    shares = exchange(share.reshape(dev_count, 8 * tok_dev, model // 8), 2)
    attn = jnp.sum(shares.astype(jnp.float32), axis=0).reshape(tok_dev, model)
    stream = residual.astype(jnp.float32) + attn
    normed = (
        stream * lax.rsqrt(jnp.mean(stream * stream, axis=-1, keepdims=True) + 1e-06) * norm_gain
    ).astype(jnp.bfloat16)
    token_map = jnp.arange(pairs)[:, None] // topk == jnp.arange(tok_dev)[None, :]
    own_ids = route_ids.reshape(pairs)
    own_slots = slot_table(own_ids, EXPERTS)
    own_chosen = (own_ids[None, None, :] == jnp.arange(EXPERTS)[:, None, None]) & (
        own_slots[None, None, :] == jnp.arange(capacity)[None, :, None]
    )
    picker = jnp.einsum(
        "ecq,qt->ect",
        own_chosen.astype(jnp.bfloat16),
        token_map.astype(jnp.bfloat16),
        preferred_element_type=jnp.float32,
    ).astype(jnp.bfloat16)
    picked = jnp.dot(
        picker.reshape(EXPERTS * capacity, tok_dev), normed, preferred_element_type=jnp.float32
    ).astype(jnp.bfloat16)
    stacked = exchange(
        picked.reshape(EXPERTS, 8 * capacity, model // 8), 3, share=split
    ).reshape(dev_count * capacity, model)
    gate = jnp.dot(stacked, w_gate, preferred_element_type=jnp.float32)
    upward = jnp.dot(stacked, w_up, preferred_element_type=jnp.float32)
    act = (jax.nn.silu(gate) * upward).astype(jnp.bfloat16)
    partial_value = jnp.dot(act, w_down, preferred_element_type=jnp.float32).astype(jnp.bfloat16)
    returned = exchange(
        partial_value.reshape(dev_count, 8 * capacity, model // 8), 4
    ).reshape(EXPERTS, split, capacity, model)
    summed = jnp.sum(returned.astype(jnp.float32), axis=1)
    weights = jnp.where(own_chosen, route_gates.reshape(1, 1, pairs), 0.0)
    mixing = jnp.einsum(
        "ecq,qt->tec", weights, token_map.astype(jnp.float32), precision=lax.Precision.HIGHEST
    )
    moe = jnp.einsum("tec,ecd->td", mixing, summed, precision=lax.Precision.HIGHEST)
    return (attn.astype(jnp.bfloat16), moe.astype(jnp.bfloat16))


def solution(mesh):
    return jax.shard_map(
        shards,
        mesh=mesh,
        in_specs=(
            P(("groups", "ep"), None),
            P("groups", "ep", None),
            P(("groups", "ep"), None),
            P(("groups", "ep"), None, None),
            P(("groups", "ep")),
            P("ep", None, None),
            P("ep", None, None),
            P("ep", None),
            P(),
            P(None, "ep"),
            P(None, "ep"),
            P("ep", None),
            P(("groups", "ep"), None),
            P(("groups", "ep"), None),
        ),
        out_specs=(P(("groups", "ep"), None), P(("groups", "ep"), None)),
        check_vma=False,
    )
```

time: 242 us -> 128 us (0.53)
  waiting for transfers between devices: 118 us -> 0 us
  Pallas kernels: 0 us -> 88.4 us
  blocking collectives: 46.8 us -> 0 us
  starting transfers between devices: 15.8 us -> 0 us
  between operations: 14.9 us -> 0.96 us
  local copies, waits for them, and re-layouts: 12.5 us -> 4.93 us
    unnamed x2 -> x0, waiting for transfers between devices: 93.6 us -> none
    pallas_call x0 -> x5, Pallas kernels: none -> 88.4 us  [exchange(): pl.pallas_call(functools.partial(exchange_kernel, n, share), out_shape=ja...]
    all_gather x2 -> x0, blocking collectives: 46.8 us -> none  [the longest x1 24.7 us: shards(): ids_every = lax.all_gather(route_ids, 'ep', axis=0, tiled=True)]
    all_to_all x3 -> x0, waiting for transfers between devices: 24.8 us -> none  [the longest x1 13.4 us: shards(): lax.all_to_all(q_abs, 'ep', split_axis=0, concat_axis=1, tiled=True)]
    all_to_all x3 -> x0, starting transfers between devices: 15.7 us -> none  [the longest x1 7.39 us: shards(): lax.all_to_all(q_abs, 'ep', split_axis=0, concat_axis=1, tiled=True)]
    dot_general x3 -> x5, matrix products: 2.62 us -> 6.17 us  [the longest x1 2.39 us: latent_attention(): jnp.einsum('grqc,rkc->rgqk', q_req, kv_cache, preferred_element_type=jnp....]
    sub x1 -> x0, matrix products: 3.21 us -> none  [latent_attention(): powers = jnp.where(valid, jnp.exp(scores - highest), 0.0)]
    unnamed x21 -> x18, local copies, waits for them, and re-layouts: 3.07 us -> 0.25 us
  transfers between devices with their start and end apart: 4 -> 0, of which waited for: 3 -> 0; matrix products, arithmetic and copies ran while one was open for 3% -> 0% of each run, Pallas kernels for 0% -> 0%
where the time goes in v1:
time: 128 us; the launch traced here: 127 us
  Pallas kernels  88.4 us (69%)
  matrix products  28.4 us (22%)
  local copies, waits for them, and re-layouts  4.93 us (4%)
  other arithmetic  3.95 us (3%)
    pallas_call x5, Pallas kernels, exchange(): pl.pallas_call(functools.partial(exchange_kernel, n, share), out_shape=ja...  88.4 us
    dot_general x1, matrix products, shards(): jnp.dot(v_flat, w_out, preferred_element_type=jnp.float32)  7.93 us
    dot_general x1, matrix products, shards(): jnp.dot(act, w_down, preferred_element_type=jnp.float32)  7.89 us
    dot_general x1, matrix products, shards(): gate = jnp.dot(stacked, w_gate, preferred_element_type=jnp.float32)  4.42 us

profile of v1, /device:TPU:0, one launch (start us, length us, event | category | flops | bytes accessed | tf_op | source)
XLA Modules:
  0.0 126.7 jit_solution(6594238070223929198)
XLA Ops:
  0.6 0.0 copy-start
  0.6 0.0 copy-start.4
  0.7 0.8 iota_compare_fusion.2
  1.5 0.9 slice.24
  2.4 0.0 copy-done
  2.4 0.3 fusion.5
  2.7 0.9 slice.25
  3.6 0.1 pad_maximum_fusion
  3.7 0.4 copy.54
  4.1 0.0 copy-start.1
  4.1 17.5 %shard_map.149 = bf16[16,32,576]{2,1,0:T(8,128)(2,1)S(1)} custom-call(bf16[16,32,576]{2,1,0:T(8,128)(2,1)S(1)} %bitcast.72), custom_call_target="tpu_custom_call" | custom-call | tf_op jit(solution)/shard_map/pallas_call | solution.py:88
  21.6 2.4 %fusion.55 = (f32[2,16,16]{2,1,0:T(8,128)}, f32[2,16,16,384]{3,2,1,0:T(8,128)S(1)}) fusion(bf16[2,384,576]{1,2,0:T(8,128)(2,1)} %param.17, bf16[16,2,16,576]{3,2,1,0:T(8,128)(2,1)S(1)} %bitcast.75, pred[2,384]{1,0:T(4,128)(4,1)S(1)} %iota_compare_fusion.2), kind=kOutput, calls=%fused_computation.93 | convolution fusion | flops 227081728 | bytes 2263808 | tf_op jit(solution)/shard_map/grqc,rkc->rgqk/dot_general | solution.py:19
  24.0 0.0 copy-done.4
  24.0 0.6 reshape.221
  24.6 1.7 %fusion.56 = (f32[2,16,16]{2,1,0:T(8,128)S(1)}, f32[2,16,16,2]{2,3,1,0:T(2,128)S(1)}) fusion(bf16[2,2,576,1]{2,1,0,3:T(2,128)(2,1)} %reshape.221, bf16[16,2,16,576]{3,2,1,0:T(8,128)(2,1)S(1)} %bitcast.76, pred[16,2]{0,1:T(4,128)(4,1)S(1)} %iota_compare_fusion.5), kind=kOutput, calls=%fused_computation.94 | convolution fusion | flops 1182208 | bytes 600608 | tf_op jit(solution)/shard_map/grqc,rkc->rgqk/dot_general | solution.py:20
  26.4 0.7 max.8
  27.1 0.1 fusion.47
  27.2 0.3 fusion.12
  27.6 1.6 %fusion.3 = bf16[16,2,16,512]{3,2,0,1:T(8,128)(2,1)S(1)} fusion(bf16[2,384,576]{1,2,0:T(8,128)(2,1)} %param.17, f32[2,512]{1,0:T(2,128)S(1)} %get-tuple-element.14, f32[16,2,16]{2,0,1:T(8,128)S(1)} %bitcast.79, f32[2,512]{1,0:T(2,128)S(1)} %get-tuple-element.15, f32[16,2,16]{2,0,1:T(8,128)S(1)} %bitcast.78, f32[2,16,16,384]{3,2,1,0:T(8,128)S(1)} %get-tuple-element.11, ...), kind=kOutput, calls=%fused_computation.9 | convolution fusion | flops 203423744 | bytes 2114304 | tf_op jit(solution)/shard_map/rgqk,rkc->rgqc/dot_general | solution.py:34
  29.3 16.8 %shard_map.150 = bf16[16,32,512]{2,1,0:T(8,128)(2,1)S(1)} custom-call(bf16[16,32,512]{2,1,0:T(8,128)(2,1)S(1)} %bitcast.73), custom_call_target="tpu_custom_call" | custom-call | tf_op jit(solution)/shard_map/pallas_call | solution.py:88
  46.1 0.0 copy-done.1
  46.1 0.4 fusion.6
  46.5 0.0 copy-start.2
  46.5 0.0 copy-start.5
  46.5 0.0 copy-start.3
  46.5 7.9 %convolution_convert_fusion = bf16[64,7168]{1,0:T(8,128)(2,1)S(1)} fusion(bf16[1024,7168]{1,0:T(8,128)(2,1)} %param.21, bf16[8,8,8,128]{3,2,1,0:T(8,128)(2,1)S(1)} %fusion.6), kind=kOutput, calls=%fused_computation | convolution fusion | flops 939982848 | bytes 15728640 | tf_op jit(solution)/shard_map/dot_general | solution.py:147
  54.4 0.4 reshape.212.in_ref
  54.9 22.5 %shard_map.151 = bf16[16,32,896]{2,1,0:T(8,128)(2,1)S(1)} custom-call(bf16[16,32,896]{2,1,0:T(8,128)(2,1)S(1)} %reshape.212.in_ref), custom_call_target="tpu_custom_call" | custom-call | tf_op jit(solution)/shard_map/pallas_call | solution.py:88
  77.3 0.1 convert_reduce_fusion
  77.5 0.0 copy-done.2
  77.5 0.8 multiply_reduce_fusion
  78.3 0.0 copy-done.5
  78.3 0.1 copy.61
  78.4 0.1 eq.73
  78.5 0.1 iota_compare_fusion.1
  78.6 0.2 select_reduce_fusion
  78.8 0.1 convolution_convert_fusion.5
  78.9 0.1 copy.63
  79.0 0.0 copy-done.3
  79.0 0.3 convolution_convert_fusion.2
  79.3 0.1 reshape.215.in_ref
  79.4 17.0 %shard_map.152 = bf16[16,16,896]{2,1,0:T(8,128)(2,1)S(1)} custom-call(bf16[8,16,896]{2,1,0:T(8,128)(2,1)S(1)} %reshape.215.in_ref), custom_call_target="tpu_custom_call" | custom-call | tf_op jit(solution)/shard_map/pallas_call | solution.py:88
  96.4 0.2 reshape.216
  96.6 4.4 %fusion.57 = f32[32,512]{1,0:T(8,128)S(1)} fusion(bf16[32,7168]{1,0:T(8,128)(2,1)S(1)} %reshape.216, bf16[7168,512]{1,0:T(8,128)(2,1)} %param.23), kind=kOutput, calls=%fused_computation.95 | convolution fusion | flops 234881024 | bytes 7864320 | tf_op jit(solution)/shard_map/dot_general | solution.py:172
  101.0 0.0 copy-start.6
  101.0 7.9 %convolution_convert_fusion.1 = bf16[32,7168]{1,0:T(8,128)(2,1)S(1)} fusion(bf16[512,7168]{1,0:T(8,128)(2,1)} %param.25, bf16[32,7168]{1,0:T(8,128)(2,1)S(1)} %reshape.216, bf16[7168,512]{1,0:T(8,128)(2,1)} %param.24, f32[32,512]{1,0:T(8,128)S(1)} %fusion.57), kind=kOutput, calls=%fused_computation.1 | convolution fusion | flops 470089728 | bytes 15663104 | tf_op jit(solution)/shard_map/dot_general | solution.py:175
  108.9 0.2 reshape.217.in_ref
  109.2 14.8 %shard_map.153 = bf16[16,16,896]{2,1,0:T(8,128)(2,1)S(1)} custom-call(bf16[16,16,896]{2,1,0:T(8,128)(2,1)S(1)} %reshape.217.in_ref), custom_call_target="tpu_custom_call" | custom-call | tf_op jit(solution)/shard_map/pallas_call | solution.py:88
  124.0 0.5 reshape.219
  124.5 0.7 reduce_sum.59
  125.2 0.0 copy-done.6
  125.2 0.1 copy.62
  125.3 0.1 broadcast_in_dim.77
  125.4 0.1 fusion.34
  125.5 1.2 fusion
  (16 shorter events, 0.3 us)
Async XLA Ops:
  0.6 1.8 %copy-start = (bf16[8,128,512]{2,1,0:T(8,128)(2,1)S(1)}, bf16[8,128,512]{2,1,0:T(8,128)(2,1)}, u32[]{:S(2)}) copy-start(bf16[8,128,512]{2,1,0:T(8,128)(2,1)} %param.19) | copy-start | bytes 3145732
  0.6 23.4 %copy-start.4 = (bf16[4,576]{1,0:T(4,128)(2,1)S(1)}, bf16[4,576]{1,0:T(4,128)(2,1)}, u32[]{:S(2)}) copy-start(bf16[4,576]{1,0:T(4,128)(2,1)} %param.16) | copy-start | bytes 13828
  4.1 41.9 %copy-start.1 = (bf16[8,512,128]{2,1,0:T(8,128)(2,1)S(1)}, bf16[8,512,128]{2,1,0:T(8,128)(2,1)}, u32[]{:S(2)}) copy-start(bf16[8,512,128]{2,1,0:T(8,128)(2,1)} %param.20) | copy-start | bytes 3145732
  46.5 31.1 %copy-start.2 = (bf16[4,7168]{1,0:T(4,128)(2,1)S(1)}, bf16[4,7168]{1,0:T(4,128)(2,1)}, u32[]{:S(2)}) copy-start(bf16[4,7168]{1,0:T(4,128)(2,1)} %param.14) | copy-start | bytes 172036
  46.5 31.8 %copy-start.5 = (s32[4,2]{0,1:T(2,128)S(1)}, s32[4,2]{0,1:T(2,128)}, u32[]{:S(2)}) copy-start(s32[4,2]{0,1:T(2,128)} %param.26) | copy-start | bytes 100
  46.5 32.6 %copy-start.3 = (f32[7168]{0:T(1024)S(1)}, f32[7168]{0:T(1024)}, u32[]{:S(2)}) copy-start(f32[7168]{0:T(1024)} %param.22) | copy-start | bytes 86020
  101.0 24.1 %copy-start.6 = (f32[4,2]{0,1:T(2,128)S(1)}, f32[4,2]{0,1:T(2,128)}, u32[]{:S(2)}) copy-start(f32[4,2]{0,1:T(2,128)} %param.27) | copy-start | bytes 100

commit v2 on v1

--- a/solution.py
+++ b/solution.py
@@ -40,7 +40,7 @@
     return jnp.transpose(latent, (1, 0, 2, 3)).reshape(groups, rows, lat_width)
 
 
-def exchange_kernel(n, share, in_ref, out_ref, send_sem, recv_sem, own_sem):
+def exchange_kernel(n, in_ref, out_ref, send_sem, recv_sem, own_sem):
     me = lax.axis_index("ep")
     barrier = pltpu.get_barrier_semaphore()
 
@@ -54,14 +54,14 @@
         return carry
 
     lax.fori_loop(1, n, greet, 0)
-    own = pltpu.make_async_copy(in_ref.at[me // share], out_ref.at[me], own_sem)
+    own = pltpu.make_async_copy(in_ref.at[me], out_ref.at[me], own_sem)
     own.start()
     pl.semaphore_wait(barrier, n - 1)
 
     def copy(k):
         target = lax.rem(me + k, n)
         return pltpu.make_async_remote_copy(
-            src_ref=in_ref.at[target // share],
+            src_ref=in_ref.at[target],
             dst_ref=out_ref.at[me],
             send_sem=send_sem.at[k],
             recv_sem=recv_sem.at[k],
@@ -82,12 +82,11 @@
     lax.fori_loop(1, n, finish, 0)
 
 
-def exchange(blocks, number, share=1):
-    n = blocks.shape[0] * share
-    shape = (n,) + blocks.shape[1:]
+def exchange(blocks, number):
+    n = blocks.shape[0]
     return pl.pallas_call(
-        functools.partial(exchange_kernel, n, share),
-        out_shape=jax.ShapeDtypeStruct(shape, blocks.dtype),
+        functools.partial(exchange_kernel, n),
+        out_shape=jax.ShapeDtypeStruct(blocks.shape, blocks.dtype),
         in_specs=[pl.BlockSpec(memory_space=pltpu.VMEM)],
         out_specs=pl.BlockSpec(memory_space=pltpu.VMEM),
         scratch_shapes=[
@@ -95,6 +94,194 @@
             pltpu.SemaphoreType.DMA((n,)),
             pltpu.SemaphoreType.DMA,
         ],
+        compiler_params=pltpu.CompilerParams(
+            collective_id=number, has_side_effects=True, vmem_limit_bytes=32 * 2**20
+        ),
+    )(blocks)
+
+
+MESH = pl.DeviceIdType.MESH
+
+
+def places(half):
+    me = lax.axis_index("ep")
+    chip, core = me // 2, lax.rem(me, 2)
+    return me, chip, core, chip * 2 + 1 - core
+
+
+def greet_peers(half, chip, core, partner):
+    barrier = pltpu.get_barrier_semaphore()
+
+    def greet(k, carry):
+        pl.semaphore_signal(
+            barrier,
+            inc=1,
+            device_id={"ep": lax.rem(chip + k, half) * 2 + core},
+            device_id_type=MESH,
+        )
+        return carry
+
+    pl.semaphore_signal(barrier, inc=1, device_id={"ep": partner}, device_id_type=MESH)
+    lax.fori_loop(1, half, greet, 0)
+    pl.semaphore_wait(barrier, half)
+
+
+def pair_sum_kernel(
+    half, final, in_ref, out_ref, paired, summed, landed, pair_send, pair_recv, send_sem, recv_sem
+):
+    me, chip, core, partner = places(half)
+    greet_peers(half, chip, core, partner)
+    place = landed if final else out_ref
+
+    def pair_copy(k):
+        at = lax.rem(chip + k, half)
+        return pltpu.make_async_remote_copy(
+            src_ref=in_ref.at[at * 2 + 1 - core],
+            dst_ref=paired.at[at],
+            send_sem=pair_send.at[k],
+            recv_sem=pair_recv.at[k],
+            device_id={"ep": partner},
+            device_id_type=MESH,
+        )
+
+    def chip_copy(k):
+        at = lax.rem(chip + k, half)
+        return pltpu.make_async_remote_copy(
+            src_ref=summed.at[at],
+            dst_ref=place.at[chip],
+            send_sem=send_sem.at[k],
+            recv_sem=recv_sem.at[k],
+            device_id={"ep": at * 2 + core},
+            device_id_type=MESH,
+        )
+
+    def add(at):
+        return in_ref[at * 2 + core].astype(jnp.float32) + paired[at].astype(jnp.float32)
+
+    def begin(k, carry):
+        pair_copy(lax.rem(k, half)).start()
+        return carry
+
+    def pass_on(k, carry):
+        pair_copy(k).wait_recv()
+        at = lax.rem(chip + k, half)
+        summed[at] = add(at).astype(summed.dtype)
+        chip_copy(k).start()
+        return carry
+
+    lax.fori_loop(1, half + 1, begin, 0)
+    lax.fori_loop(1, half, pass_on, 0)
+    pair_copy(0).wait_recv()
+    if final:
+        out_ref[...] = add(chip)
+
+        def collect(k, carry):
+            chip_copy(k).wait_recv()
+            out_ref[...] += landed[lax.rem(chip + half - k, half)].astype(jnp.float32)
+            return carry
+
+    else:
+        out_ref[chip] = add(chip).astype(out_ref.dtype)
+
+        def collect(k, carry):
+            chip_copy(k).wait_recv()
+            return carry
+
+    def finish(k, carry):
+        pair_copy(k).wait_send()
+        return carry
+
+    def finish_chip(k, carry):
+        chip_copy(k).wait_send()
+        return carry
+
+    lax.fori_loop(1, half, collect, 0)
+    lax.fori_loop(0, half, finish, 0)
+    lax.fori_loop(1, half, finish_chip, 0)
+
+
+def pair_sum_exchange(blocks, number, final):
+    n, rows, columns = blocks.shape
+    half = n // 2
+    kind = jnp.float32 if final else blocks.dtype
+    shape = (rows, columns) if final else (half, rows, columns)
+    buffer = pltpu.VMEM((half, rows, columns), blocks.dtype)
+    return pl.pallas_call(
+        functools.partial(pair_sum_kernel, half, final),
+        out_shape=jax.ShapeDtypeStruct(shape, kind),
+        in_specs=[pl.BlockSpec(memory_space=pltpu.VMEM)],
+        out_specs=pl.BlockSpec(memory_space=pltpu.VMEM),
+        scratch_shapes=[buffer, buffer, buffer] + [pltpu.SemaphoreType.DMA((half,))] * 4,
+        compiler_params=pltpu.CompilerParams(
+            collective_id=number, has_side_effects=True, vmem_limit_bytes=32 * 2**20
+        ),
+    )(blocks)
+
+
+def dispatch_kernel(
+    half, share, in_ref, out_ref, send_sem, recv_sem, pass_send, pass_recv, own_sem
+):
+    me, chip, core, partner = places(half)
+    own = pltpu.make_async_copy(in_ref.at[chip // share], out_ref.at[me], own_sem)
+    own.start()
+    greet_peers(half, chip, core, partner)
+
+    def chip_copy(k):
+        at = lax.rem(chip + k, half)
+        return pltpu.make_async_remote_copy(
+            src_ref=in_ref.at[at // share],
+            dst_ref=out_ref.at[me],
+            send_sem=send_sem.at[k],
+            recv_sem=recv_sem.at[k],
+            device_id={"ep": at * 2 + core},
+            device_id_type=MESH,
+        )
+
+    def pass_copy(k):
+        source = lax.rem(chip + half - k, half) * 2 + core
+        return pltpu.make_async_remote_copy(
+            src_ref=out_ref.at[source],
+            dst_ref=out_ref.at[source],
+            send_sem=pass_send.at[k],
+            recv_sem=pass_recv.at[k],
+            device_id={"ep": partner},
+            device_id_type=MESH,
+        )
+
+    def begin(k, carry):
+        chip_copy(k).start()
+        return carry
+
+    def pass_on(k, carry):
+        chip_copy(k).wait_recv()
+        pass_copy(k).start()
+        return carry
+
+    def finish(k, carry):
+        chip_copy(k).wait_send()
+        return carry
+
+    def finish_pass(k, carry):
+        pass_copy(k).wait()
+        return carry
+
+    lax.fori_loop(1, half, begin, 0)
+    own.wait()
+    pass_copy(0).start()
+    lax.fori_loop(1, half, pass_on, 0)
+    lax.fori_loop(1, half, finish, 0)
+    lax.fori_loop(0, half, finish_pass, 0)
+
+
+def dispatch(blocks, number, half):
+    share = half // blocks.shape[0]
+    shape = (2 * half,) + blocks.shape[1:]
+    return pl.pallas_call(
+        functools.partial(dispatch_kernel, half, share),
+        out_shape=jax.ShapeDtypeStruct(shape, blocks.dtype),
+        in_specs=[pl.BlockSpec(memory_space=pltpu.VMEM)],
+        out_specs=pl.BlockSpec(memory_space=pltpu.VMEM),
+        scratch_shapes=[pltpu.SemaphoreType.DMA((half,))] * 4 + [pltpu.SemaphoreType.DMA],
         compiler_params=pltpu.CompilerParams(
             collective_id=number, has_side_effects=True, vmem_limit_bytes=32 * 2**20
         ),
@@ -145,8 +332,8 @@
     ).astype(jnp.bfloat16)
     v_flat = v_out.reshape(v_out.shape[0], v_out.shape[1] * v_out.shape[2])
     share = jnp.dot(v_flat, w_out, preferred_element_type=jnp.float32).astype(jnp.bfloat16)
-    shares = exchange(share.reshape(dev_count, 8 * tok_dev, model // 8), 2)
-    attn = jnp.sum(shares.astype(jnp.float32), axis=0).reshape(tok_dev, model)
+    blocks = share.reshape(dev_count, 8 * tok_dev, model // 8)
+    attn = pair_sum_exchange(blocks, 2, True).reshape(tok_dev, model)
     stream = residual.astype(jnp.float32) + attn
     normed = (
         stream * lax.rsqrt(jnp.mean(stream * stream, axis=-1, keepdims=True) + 1e-06) * norm_gain
@@ -166,16 +353,16 @@
     picked = jnp.dot(
         picker.reshape(EXPERTS * capacity, tok_dev), normed, preferred_element_type=jnp.float32
     ).astype(jnp.bfloat16)
-    stacked = exchange(
-        picked.reshape(EXPERTS, 8 * capacity, model // 8), 3, share=split
+    stacked = dispatch(
+        picked.reshape(EXPERTS, 8 * capacity, model // 8), 3, dev_count // 2
     ).reshape(dev_count * capacity, model)
     gate = jnp.dot(stacked, w_gate, preferred_element_type=jnp.float32)
     upward = jnp.dot(stacked, w_up, preferred_element_type=jnp.float32)
     act = (jax.nn.silu(gate) * upward).astype(jnp.bfloat16)
     partial_value = jnp.dot(act, w_down, preferred_element_type=jnp.float32).astype(jnp.bfloat16)
-    returned = exchange(
-        partial_value.reshape(dev_count, 8 * capacity, model // 8), 4
-    ).reshape(EXPERTS, split, capacity, model)
+    returned = pair_sum_exchange(
+        partial_value.reshape(dev_count, 8 * capacity, model // 8), 4, False
+    ).reshape(EXPERTS, split // 2, capacity, model)
     summed = jnp.sum(returned.astype(jnp.float32), axis=1)
     weights = jnp.where(own_chosen, route_gates.reshape(1, 1, pairs), 0.0)
     mixing = jnp.einsum(

time: 128 us -> 111 us (0.87); the launches traced: 127 us -> 111 us
  Pallas kernels: 88.4 us -> 74.3 us
    pallas_call x5, Pallas kernels: 88.4 us -> 74.3 us  [the longest x2 34.2 us: exchange(): pl.pallas_call(functools.partial(exchange_kernel, n), out_shape=jax.Shape...]
where the time goes in v2:
time: 111 us
  Pallas kernels  74.3 us (67%)
  matrix products  28.2 us (25%)
  local copies, waits for them, and re-layouts  4.5 us (4%)
  other arithmetic  3.1 us (3%)
    pallas_call x2, Pallas kernels, exchange(): pl.pallas_call(functools.partial(exchange_kernel, n), out_shape=jax.Shape...  34.2 us
    pallas_call x2, Pallas kernels, pair_sum_exchange(): pl.pallas_call(functools.partial(pair_sum_kernel, half, final), out_shape...  27.3 us
    pallas_call x1, Pallas kernels, dispatch(): pl.pallas_call(functools.partial(dispatch_kernel, half, share), out_shape...  12.7 us
    dot_general x1, matrix products, shards(): jnp.dot(v_flat, w_out, preferred_element_type=jnp.float32)  7.93 us
    dot_general x1, matrix products, shards(): jnp.dot(act, w_down, preferred_element_type=jnp.float32)  7.89 us
    dot_general x1, matrix products, shards(): gate = jnp.dot(stacked, w_gate, preferred_element_type=jnp.float32)  4.42 us
    dot_general x1, matrix products, latent_attention(): jnp.einsum('grqc,rkc->rgqk', q_req, kv_cache, preferred_element_type=jnp....  2.39 us

profile of v2, /device:TPU:0, one launch (start us, length us, event | category | flops | bytes accessed | tf_op | source)
XLA Modules:
  0.0 111.1 jit_solution(9640666184159465974)
XLA Ops:
  0.6 0.0 copy-start
  0.6 0.0 copy-start.4
  0.7 0.8 iota_compare_fusion.2
  1.5 0.9 slice.24
  2.4 0.0 copy-done
  2.4 0.3 fusion.5
  2.7 0.9 slice.25
  3.6 0.1 pad_maximum_fusion
  3.7 0.4 copy.43
  4.1 0.0 copy-start.1
  4.1 17.5 %shard_map.149 = bf16[16,32,576]{2,1,0:T(8,128)(2,1)S(1)} custom-call(bf16[16,32,576]{2,1,0:T(8,128)(2,1)S(1)} %bitcast.72), custom_call_target="tpu_custom_call" | custom-call | tf_op jit(solution)/shard_map/pallas_call | solution.py:87
  21.6 2.4 %fusion.55 = (f32[2,16,16]{2,1,0:T(8,128)}, f32[2,16,16,384]{3,2,1,0:T(8,128)S(1)}) fusion(bf16[2,384,576]{1,2,0:T(8,128)(2,1)} %param.17, bf16[16,2,16,576]{3,2,1,0:T(8,128)(2,1)S(1)} %bitcast.75, pred[2,384]{1,0:T(4,128)(4,1)S(1)} %iota_compare_fusion.2), kind=kOutput, calls=%fused_computation.92 | convolution fusion | flops 227081728 | bytes 2263808 | tf_op jit(solution)/shard_map/grqc,rkc->rgqk/dot_general | solution.py:19
  24.0 0.0 copy-done.4
  24.0 0.6 reshape.220
  24.6 1.7 %fusion.56 = (f32[2,16,16]{2,1,0:T(8,128)S(1)}, f32[2,16,16,2]{2,3,1,0:T(2,128)S(1)}) fusion(bf16[2,2,576,1]{2,1,0,3:T(2,128)(2,1)} %reshape.220, bf16[16,2,16,576]{3,2,1,0:T(8,128)(2,1)S(1)} %bitcast.76, pred[16,2]{0,1:T(4,128)(4,1)S(1)} %iota_compare_fusion.5), kind=kOutput, calls=%fused_computation.93 | convolution fusion | flops 1182208 | bytes 600608 | tf_op jit(solution)/shard_map/grqc,rkc->rgqk/dot_general | solution.py:20
  26.4 0.7 max.8
  27.1 0.1 fusion.47
  27.2 0.3 fusion.12
  27.6 1.6 %fusion.3 = bf16[16,2,16,512]{3,2,0,1:T(8,128)(2,1)S(1)} fusion(bf16[2,384,576]{1,2,0:T(8,128)(2,1)} %param.17, f32[2,512]{1,0:T(2,128)S(1)} %get-tuple-element.14, f32[16,2,16]{2,0,1:T(8,128)S(1)} %bitcast.79, f32[2,512]{1,0:T(2,128)S(1)} %get-tuple-element.15, f32[16,2,16]{2,0,1:T(8,128)S(1)} %bitcast.78, f32[2,16,16,384]{3,2,1,0:T(8,128)S(1)} %get-tuple-element.11, ...), kind=kOutput, calls=%fused_computation.8 | convolution fusion | flops 203423744 | bytes 2114304 | tf_op jit(solution)/shard_map/rgqk,rkc->rgqc/dot_general | solution.py:34
  29.3 16.8 %shard_map.150 = bf16[16,32,512]{2,1,0:T(8,128)(2,1)S(1)} custom-call(bf16[16,32,512]{2,1,0:T(8,128)(2,1)S(1)} %bitcast.73), custom_call_target="tpu_custom_call" | custom-call | tf_op jit(solution)/shard_map/pallas_call | solution.py:87
  46.1 0.0 copy-done.1
  46.1 0.4 fusion.6
  46.5 0.0 copy-start.2
  46.5 0.0 copy-start.5
  46.5 0.0 copy-start.3
  46.5 7.9 %convolution_convert_fusion = bf16[64,7168]{1,0:T(8,128)(2,1)S(1)} fusion(bf16[1024,7168]{1,0:T(8,128)(2,1)} %param.21, bf16[8,8,8,128]{3,2,1,0:T(8,128)(2,1)S(1)} %fusion.6), kind=kOutput, calls=%fused_computation | convolution fusion | flops 939982848 | bytes 15728640 | tf_op jit(solution)/shard_map/dot_general | solution.py:334
  54.4 0.4 reshape.212.in_ref
  54.9 16.3 %shard_map.151 = f32[32,896]{1,0:T(8,128)S(1)} custom-call(bf16[16,32,896]{2,1,0:T(8,128)(2,1)S(1)} %reshape.212.in_ref), custom_call_target="tpu_custom_call" | custom-call | tf_op jit(solution)/shard_map/pallas_call | solution.py:209
  71.2 0.0 copy-done.2
  71.2 0.8 multiply_reduce_fusion
  72.0 0.0 copy-done.5
  72.0 0.1 copy.50
  72.1 0.1 eq.73
  72.2 0.1 iota_compare_fusion.1
  72.3 0.2 select_reduce_fusion
  72.5 0.1 convolution_convert_fusion.5
  72.6 0.1 copy.52
  72.7 0.0 copy-done.3
  72.7 0.3 convolution_convert_fusion.2
  73.0 0.1 reshape.215.in_ref
  73.1 12.7 %shard_map.152 = bf16[16,16,896]{2,1,0:T(8,128)(2,1)S(1)} custom-call(bf16[8,16,896]{2,1,0:T(8,128)(2,1)S(1)} %reshape.215.in_ref), custom_call_target="tpu_custom_call" | custom-call | tf_op jit(solution)/shard_map/pallas_call | solution.py:279
  85.9 0.2 reshape.216
  86.1 4.4 %fusion.57 = f32[32,512]{1,0:T(8,128)S(1)} fusion(bf16[32,7168]{1,0:T(8,128)(2,1)S(1)} %reshape.216, bf16[7168,512]{1,0:T(8,128)(2,1)} %param.23), kind=kOutput, calls=%fused_computation.94 | convolution fusion | flops 234881024 | bytes 7864320 | tf_op jit(solution)/shard_map/dot_general | solution.py:359
  90.5 0.0 copy-start.6
  90.5 7.9 %convolution_convert_fusion.1 = bf16[32,7168]{1,0:T(8,128)(2,1)S(1)} fusion(bf16[512,7168]{1,0:T(8,128)(2,1)} %param.25, bf16[32,7168]{1,0:T(8,128)(2,1)S(1)} %reshape.216, bf16[7168,512]{1,0:T(8,128)(2,1)} %param.24, f32[32,512]{1,0:T(8,128)S(1)} %fusion.57), kind=kOutput, calls=%fused_computation.1 | convolution fusion | flops 470089728 | bytes 15663104 | tf_op jit(solution)/shard_map/dot_general | solution.py:362
  98.4 0.2 reshape.217.in_ref
  98.7 11.0 %shard_map.153 = bf16[8,16,896]{2,1,0:T(8,128)(2,1)S(1)} custom-call(bf16[16,16,896]{2,1,0:T(8,128)(2,1)S(1)} %reshape.217.in_ref), custom_call_target="tpu_custom_call" | custom-call | tf_op jit(solution)/shard_map/pallas_call | solution.py:209
  109.7 0.1 reduce_sum.46
  109.8 0.0 copy-done.6
  109.8 0.1 copy.51
  109.9 0.1 broadcast_in_dim.77
  110.0 0.1 fusion.34
  110.1 1.0 fusion
  (16 shorter events, 0.3 us)
Async XLA Ops:
  0.6 1.8 %copy-start = (bf16[8,128,512]{2,1,0:T(8,128)(2,1)S(1)}, bf16[8,128,512]{2,1,0:T(8,128)(2,1)}, u32[]{:S(2)}) copy-start(bf16[8,128,512]{2,1,0:T(8,128)(2,1)} %param.19) | copy-start | bytes 3145732
  0.6 23.4 %copy-start.4 = (bf16[4,576]{1,0:T(4,128)(2,1)S(1)}, bf16[4,576]{1,0:T(4,128)(2,1)}, u32[]{:S(2)}) copy-start(bf16[4,576]{1,0:T(4,128)(2,1)} %param.16) | copy-start | bytes 13828
  4.1 41.9 %copy-start.1 = (bf16[8,512,128]{2,1,0:T(8,128)(2,1)S(1)}, bf16[8,512,128]{2,1,0:T(8,128)(2,1)}, u32[]{:S(2)}) copy-start(bf16[8,512,128]{2,1,0:T(8,128)(2,1)} %param.20) | copy-start | bytes 3145732
  46.5 24.8 %copy-start.2 = (bf16[4,7168]{1,0:T(4,128)(2,1)S(1)}, bf16[4,7168]{1,0:T(4,128)(2,1)}, u32[]{:S(2)}) copy-start(bf16[4,7168]{1,0:T(4,128)(2,1)} %param.14) | copy-start | bytes 172036
  46.5 25.5 %copy-start.5 = (s32[4,2]{0,1:T(2,128)S(1)}, s32[4,2]{0,1:T(2,128)}, u32[]{:S(2)}) copy-start(s32[4,2]{0,1:T(2,128)} %param.26) | copy-start | bytes 100
  46.5 26.3 %copy-start.3 = (f32[7168]{0:T(1024)S(1)}, f32[7168]{0:T(1024)}, u32[]{:S(2)}) copy-start(f32[7168]{0:T(1024)} %param.22) | copy-start | bytes 86020
  90.5 19.2 %copy-start.6 = (f32[4,2]{0,1:T(2,128)S(1)}, f32[4,2]{0,1:T(2,128)}, u32[]{:S(2)}) copy-start(f32[4,2]{0,1:T(2,128)} %param.27) | copy-start | bytes 100

commit v3 on v2

--- a/solution.py
+++ b/solution.py
@@ -101,6 +101,138 @@
 
 
 MESH = pl.DeviceIdType.MESH
+TOGETHER = 4
+FRESH_ROWS = 16
+
+
+def attend_kernel(
+    n,
+    scale,
+    q_ref,
+    cache_ref,
+    fresh_ref,
+    keep_ref,
+    out_ref,
+    landed,
+    latents,
+    send_sem,
+    recv_sem,
+    back_send,
+    back_recv,
+):
+    me = lax.axis_index("ep")
+    requests, lat_width = cache_ref.shape[0], out_ref.shape[2]
+    part = q_ref.shape[1] // requests
+    barrier = pltpu.get_barrier_semaphore()
+
+    def greet(k, carry):
+        pl.semaphore_signal(
+            barrier, inc=1, device_id={"ep": lax.rem(me + k, n)}, device_id_type=MESH
+        )
+        return carry
+
+    def copy(k):
+        target = lax.rem(me + k, n)
+        return pltpu.make_async_remote_copy(
+            src_ref=q_ref.at[target],
+            dst_ref=landed.at[me],
+            send_sem=send_sem.at[k],
+            recv_sem=recv_sem.at[k],
+            device_id={"ep": target},
+            device_id_type=MESH,
+        )
+
+    def back(k):
+        source = lax.rem(me + n - k, n)
+        return pltpu.make_async_remote_copy(
+            src_ref=latents.at[source],
+            dst_ref=out_ref.at[me],
+            send_sem=back_send.at[k],
+            recv_sem=back_recv.at[k],
+            device_id={"ep": source},
+            device_id_type=MESH,
+        )
+
+    def attend(sources):
+        count = len(sources) * part
+        shape = (count, FRESH_ROWS)
+        draft = lax.rem(lax.broadcasted_iota(jnp.int32, shape, 0), part) // (part // 2)
+        keep_new = lax.broadcasted_iota(jnp.int32, shape, 1) <= draft
+        for r in range(requests):
+            rows = pl.ds(r * part, part)
+            q = jnp.concatenate([landed[s, rows, :] for s in sources], axis=0)
+            keys, fresh = cache_ref[r], fresh_ref[r]
+            contract = (((1,), (1,)), ((), ()))
+            old = lax.dot_general(q, keys, contract, preferred_element_type=jnp.float32)
+            new = lax.dot_general(q, fresh, contract, preferred_element_type=jnp.float32)
+            keep_old = jnp.broadcast_to(keep_ref[r], old.shape) > 0.5
+            old = jnp.where(keep_old, old * scale, -1e30)
+            new = jnp.where(keep_new, new * scale, -1e30)
+            highest = jnp.maximum(
+                jnp.max(old, axis=1, keepdims=True), jnp.max(new, axis=1, keepdims=True)
+            )
+            old = jnp.where(keep_old, jnp.exp(old - highest), 0.0)
+            new = jnp.where(keep_new, jnp.exp(new - highest), 0.0)
+            total = jnp.sum(old, axis=1, keepdims=True) + jnp.sum(new, axis=1, keepdims=True)
+            old = (old / total).astype(jnp.bfloat16)
+            new = (new / total).astype(jnp.bfloat16)
+            latent = jnp.dot(old, keys[:, :lat_width], preferred_element_type=jnp.float32)
+            latent += jnp.dot(new, fresh[:, :lat_width], preferred_element_type=jnp.float32)
+            latent = latent.astype(jnp.bfloat16)
+            for i, s in enumerate(sources):
+                latents[s, rows, :] = latent[i * part : (i + 1) * part]
+
+    def start(k, carry):
+        copy(k).start()
+        return carry
+
+    lax.fori_loop(1, n, greet, 0)
+    landed[me] = q_ref[me]
+    pl.semaphore_wait(barrier, n - 1)
+    lax.fori_loop(1, n, start, 0)
+
+    def turn(first, skip):
+        for k in range(skip, TOGETHER):
+            copy(first + k).wait_recv()
+        attend([lax.rem(me + n - first - k, n) for k in range(TOGETHER)])
+        for k in range(skip, TOGETHER):
+            back(first + k).start()
+
+    def step(group, carry):
+        turn(group * TOGETHER, 0)
+        return carry
+
+    turn(0, 1)
+    out_ref[me] = latents[me]
+    lax.fori_loop(1, n // TOGETHER, step, 0)
+
+    def finish(k, carry):
+        copy(k).wait_send()
+        back(k).wait()
+        return carry
+
+    lax.fori_loop(1, n, finish, 0)
+
+
+def attend_exchange(blocks, new_kv, kv_cache, lengths, scale, lat_width, number):
+    n, rows, width = blocks.shape
+    requests, seq_len, _ = kv_cache.shape
+    fresh = jnp.pad(new_kv.reshape(requests, 2, width), ((0, 0), (0, FRESH_ROWS - 2), (0, 0)))
+    keep = (jnp.arange(seq_len) < lengths[:, None]).astype(jnp.float32)[:, None, :]
+    return pl.pallas_call(
+        functools.partial(attend_kernel, n, scale),
+        out_shape=jax.ShapeDtypeStruct((n, rows, lat_width), blocks.dtype),
+        in_specs=[pl.BlockSpec(memory_space=pltpu.VMEM)] * 4,
+        out_specs=pl.BlockSpec(memory_space=pltpu.VMEM),
+        scratch_shapes=[
+            pltpu.VMEM((n, rows, width), blocks.dtype),
+            pltpu.VMEM((n, rows, lat_width), blocks.dtype),
+        ]
+        + [pltpu.SemaphoreType.DMA((n,))] * 4,
+        compiler_params=pltpu.CompilerParams(
+            collective_id=number, has_side_effects=True, vmem_limit_bytes=32 * 2**20
+        ),
+    )(blocks, kv_cache, fresh, keep)
 
 
 def places(half):
@@ -324,9 +456,15 @@
     ).astype(jnp.bfloat16)
     q_abs = jnp.concatenate([q_lat, queries[:, :, nope:]], axis=-1)
     heads_dev = q_abs.shape[1]
-    q_home = exchange(q_abs.reshape(dev_count, tok_dev * heads_dev, q_abs.shape[2]), 0)
-    latent = latent_attention(q_home, new_kv, kv_cache, lengths, scale, lat_width)
-    latent_heads = exchange(latent, 1).reshape(dev_count * tok_dev, heads_dev, lat_width)
+    q_blocks = q_abs.reshape(dev_count, tok_dev * heads_dev, q_abs.shape[2])
+    if (2 * heads_dev) % 16 == 0 and dev_count % TOGETHER == 0:
+        latents = attend_exchange(q_blocks, new_kv, kv_cache, lengths, scale, lat_width, 5)
+    else:
+        q_home = exchange(q_blocks, 0)
+        latents = exchange(
+            latent_attention(q_home, new_kv, kv_cache, lengths, scale, lat_width), 1
+        )
+    latent_heads = latents.reshape(dev_count * tok_dev, heads_dev, lat_width)
     v_out = jnp.einsum(
         "thc,hcv->thv", latent_heads, w_uv, preferred_element_type=jnp.float32
     ).astype(jnp.bfloat16)

time: 111 us -> 106 us (0.955)
  matrix products: 28.2 us -> 23.7 us
  local copies, waits for them, and re-layouts: 4.5 us -> 6.15 us
  Pallas kernels: 74.3 us -> 72.9 us
  other arithmetic: 3.1 us -> 1.88 us
    pallas_call x2, Pallas kernels: 27.3 us -> 20.9 us  [pair_sum_exchange(): pl.pallas_call(functools.partial(pair_sum_kernel, half, final), out_shape...]
    dot_general x3 -> x0, matrix products: 5.75 us -> none  [the longest x1 2.39 us: latent_attention(): jnp.einsum('grqc,rkc->rgqk', q_req, kv_cache, preferred_element_type=jnp....]
    pallas_call x2 -> x1, Pallas kernels: 34.2 us -> 38.7 us  [attend_exchange(): pl.pallas_call(functools.partial(attend_kernel, n, scale), out_shape=jax....]
    unnamed x18 -> x14, local copies, waits for them, and re-layouts: 0.25 us -> 1.79 us
    dot_general x1, matrix products: 0.38 us -> 1.61 us  [shards(): jnp.einsum('thc,hcv->thv', latent_heads, w_uv, preferred_element_type=jnp...]
where the time goes in v3:
time: 106 us; the launch traced here: 105 us
  Pallas kernels  72.9 us (69%)
  matrix products  23.7 us (22%)
  local copies, waits for them, and re-layouts  6.15 us (6%)
  other arithmetic  1.88 us (2%)
    pallas_call x1, Pallas kernels, attend_exchange(): pl.pallas_call(functools.partial(attend_kernel, n, scale), out_shape=jax....  38.7 us
    pallas_call x2, Pallas kernels, pair_sum_exchange(): pl.pallas_call(functools.partial(pair_sum_kernel, half, final), out_shape...  20.9 us
    pallas_call x1, Pallas kernels, dispatch(): pl.pallas_call(functools.partial(dispatch_kernel, half, share), out_shape...  13.3 us
    dot_general x1, matrix products, shards(): jnp.dot(v_flat, w_out, preferred_element_type=jnp.float32)  7.94 us
    dot_general x1, matrix products, shards(): jnp.dot(act, w_down, preferred_element_type=jnp.float32)  7.88 us
    dot_general x1, matrix products, shards(): gate = jnp.dot(stacked, w_gate, preferred_element_type=jnp.float32)  4.42 us

profile of v3, /device:TPU:0, one launch (start us, length us, event | category | flops | bytes accessed | tf_op | source)
XLA Modules:
  0.0 105.5 jit_solution(13354142870404927941)
XLA Ops:
  0.6 0.0 copy-start
  0.6 1.0 slice.7
  1.7 0.9 slice.6
  2.6 0.0 copy-done
  2.6 0.3 fusion.1
  2.9 0.1 pad_maximum_fusion
  3.0 0.4 copy.37
  3.4 1.5 %copy.38.cache_ref = bf16[2,384,576]{2,1,0:T(8,128)(2,1)S(1)} copy(bf16[2,384,576]{1,2,0:T(8,128)(2,1)} %param.17) | data formatting | bytes 1769472 | tf_op args[3]
  4.9 0.7 reshape.166
  5.6 0.7 compare_convert_fusion.keep_ref
  6.4 38.7 %shard_map.149 = bf16[16,32,512]{2,1,0:T(8,128)(2,1)S(1)} custom-call(bf16[16,32,576]{2,1,0:T(8,128)(2,1)S(1)} %bitcast.29, bf16[2,384,576]{2,1,0:T(8,128)(2,1)S(1)} %copy.38.cache_ref, bf16[2,16,576]{2,1,0:T(8,128)(2,1)S(1)} %pad.4.fresh_ref, f32[2,1,384]{2,1,0:T(1,128)S(1)} %compare_convert_fusion.keep_ref), custom_call_target="tpu_custom_call" | custom-call | tf_op jit(solution)/shard_map/pallas_call | solution.py:222
  45.1 1.6 %fusion.2 = bf16[8,8,8,128]{3,2,1,0:T(8,128)(2,1)S(1)} fusion(bf16[8,512,128]{2,1,0:T(8,128)(2,1)} %param.20, bf16[64,8,512]{2,1,0:T(8,128)(2,1)S(1)} %bitcast.30), kind=kOutput, calls=%fused_computation.8 | convolution fusion | flops 67174400 | bytes 1703936 | tf_op jit(solution)/shard_map/thc,hcv->thv/dot_general | solution.py:468
  46.7 0.0 copy-start.1
  46.7 0.0 copy-start.3
  46.7 0.0 copy-start.4
  46.8 0.0 copy-start.2
  46.8 7.9 %convolution_convert_fusion = bf16[64,7168]{1,0:T(8,128)(2,1)S(1)} fusion(bf16[1024,7168]{1,0:T(8,128)(2,1)} %param.21, bf16[8,8,8,128]{3,2,1,0:T(8,128)(2,1)S(1)} %fusion.2), kind=kOutput, calls=%fused_computation | convolution fusion | flops 939982848 | bytes 15728640 | tf_op jit(solution)/shard_map/dot_general | solution.py:472
  54.7 0.4 reshape.169.in_ref
  55.1 9.6 %shard_map.150 = f32[32,896]{1,0:T(8,128)S(1)} custom-call(bf16[16,32,896]{2,1,0:T(8,128)(2,1)S(1)} %reshape.169.in_ref), custom_call_target="tpu_custom_call" | custom-call | tf_op jit(solution)/shard_map/pallas_call | solution.py:341
  64.8 0.0 copy-done.1
  64.8 0.8 multiply_reduce_fusion
  65.6 0.0 copy-done.3
  65.6 0.1 copy.42
  65.7 0.1 broadcast_in_dim.10
  65.8 0.0 copy-done.4
  65.8 0.1 copy.41
  65.9 0.1 eq.73
  65.9 0.1 iota_compare_fusion.1
  66.0 0.2 select_reduce_fusion
  66.2 0.1 fusion.18
  66.4 0.2 convolution_convert_fusion.5
  66.6 0.1 copy.43
  66.7 0.0 copy-done.2
  66.7 0.3 convolution_convert_fusion.2
  67.0 0.1 reshape.172.in_ref
  67.1 13.3 %shard_map.151 = bf16[16,16,896]{2,1,0:T(8,128)(2,1)S(1)} custom-call(bf16[8,16,896]{2,1,0:T(8,128)(2,1)S(1)} %reshape.172.in_ref), custom_call_target="tpu_custom_call" | custom-call | tf_op jit(solution)/shard_map/pallas_call | solution.py:411
  80.4 0.2 reshape.173
  80.6 4.4 %fusion.33 = f32[32,512]{1,0:T(8,128)S(1)} fusion(bf16[32,7168]{1,0:T(8,128)(2,1)S(1)} %reshape.173, bf16[7168,512]{1,0:T(8,128)(2,1)} %param.23), kind=kOutput, calls=%fused_computation.55 | convolution fusion | flops 234881024 | bytes 7864320 | tf_op jit(solution)/shard_map/dot_general | solution.py:497
  85.1 7.9 %convolution_convert_fusion.1 = bf16[32,7168]{1,0:T(8,128)(2,1)S(1)} fusion(bf16[512,7168]{1,0:T(8,128)(2,1)} %param.25, bf16[32,7168]{1,0:T(8,128)(2,1)S(1)} %reshape.173, bf16[7168,512]{1,0:T(8,128)(2,1)} %param.24, f32[32,512]{1,0:T(8,128)S(1)} %fusion.33), kind=kOutput, calls=%fused_computation.1 | convolution fusion | flops 470089728 | bytes 15663104 | tf_op jit(solution)/shard_map/dot_general | solution.py:500
  92.9 0.2 reshape.174.in_ref
  93.2 11.3 %shard_map.152 = bf16[8,16,896]{2,1,0:T(8,128)(2,1)S(1)} custom-call(bf16[16,16,896]{2,1,0:T(8,128)(2,1)S(1)} %reshape.174.in_ref), custom_call_target="tpu_custom_call" | custom-call | tf_op jit(solution)/shard_map/pallas_call | solution.py:341
  104.5 0.1 reduce_sum.26
  104.5 0.9 fusion
  (7 shorter events, 0.1 us)
Async XLA Ops:
  0.6 2.0 %copy-start = (bf16[8,128,512]{2,1,0:T(8,128)(2,1)S(1)}, bf16[8,128,512]{2,1,0:T(8,128)(2,1)}, u32[]{:S(2)}) copy-start(bf16[8,128,512]{2,1,0:T(8,128)(2,1)} %param.19) | copy-start | bytes 3145732
  46.7 18.1 %copy-start.1 = (bf16[4,7168]{1,0:T(4,128)(2,1)S(1)}, bf16[4,7168]{1,0:T(4,128)(2,1)}, u32[]{:S(2)}) copy-start(bf16[4,7168]{1,0:T(4,128)(2,1)} %param.14) | copy-start | bytes 172036
  46.7 18.9 %copy-start.3 = (f32[4,2]{0,1:T(2,128)S(1)}, f32[4,2]{0,1:T(2,128)}, u32[]{:S(2)}) copy-start(f32[4,2]{0,1:T(2,128)} %param.27) | copy-start | bytes 100
  46.7 19.0 %copy-start.4 = (s32[4,2]{0,1:T(2,128)S(1)}, s32[4,2]{0,1:T(2,128)}, u32[]{:S(2)}) copy-start(s32[4,2]{0,1:T(2,128)} %param.26) | copy-start | bytes 100
  46.8 20.0 %copy-start.2 = (f32[7168]{0:T(1024)S(1)}, f32[7168]{0:T(1024)}, u32[]{:S(2)}) copy-start(f32[7168]{0:T(1024)} %param.22) | copy-start | bytes 86020

commit v4 on v3

--- a/solution.py
+++ b/solution.py
@@ -189,22 +189,22 @@
     lax.fori_loop(1, n, greet, 0)
     landed[me] = q_ref[me]
     pl.semaphore_wait(barrier, n - 1)
-    lax.fori_loop(1, n, start, 0)
+    lax.fori_loop(1, 2 * TOGETHER, start, 0)
 
     def turn(first, skip):
         for k in range(skip, TOGETHER):
             copy(first + k).wait_recv()
+        ahead = first + 2 * TOGETHER
+        if ahead < n:
+            lax.fori_loop(ahead, ahead + TOGETHER, start, 0)
         attend([lax.rem(me + n - first - k, n) for k in range(TOGETHER)])
         for k in range(skip, TOGETHER):
             back(first + k).start()
 
-    def step(group, carry):
-        turn(group * TOGETHER, 0)
-        return carry
-
     turn(0, 1)
     out_ref[me] = latents[me]
-    lax.fori_loop(1, n // TOGETHER, step, 0)
+    for group in range(1, n // TOGETHER):
+        turn(group * TOGETHER, 0)
 
     def finish(k, carry):
         copy(k).wait_send()
@@ -457,7 +457,7 @@
     q_abs = jnp.concatenate([q_lat, queries[:, :, nope:]], axis=-1)
     heads_dev = q_abs.shape[1]
     q_blocks = q_abs.reshape(dev_count, tok_dev * heads_dev, q_abs.shape[2])
-    if (2 * heads_dev) % 16 == 0 and dev_count % TOGETHER == 0:
+    if (2 * heads_dev) % 16 == 0 and dev_count % TOGETHER == 0 and dev_count >= 2 * TOGETHER:
         latents = attend_exchange(q_blocks, new_kv, kv_cache, lengths, scale, lat_width, 5)
     else:
         q_home = exchange(q_blocks, 0)

time: 106 us -> 106 us (level)
    pallas_call x2, Pallas kernels: 20.9 us -> 23.1 us  [pair_sum_exchange(): pl.pallas_call(functools.partial(pair_sum_kernel, half, final), out_shape...]
    pallas_call x1, Pallas kernels: 13.3 us -> 11.4 us  [dispatch(): pl.pallas_call(functools.partial(dispatch_kernel, half, share), out_shape...]
where the time goes in v4:
time: 106 us
  Pallas kernels  73.2 us (69%)
  matrix products  23.7 us (22%)
  local copies, waits for them, and re-layouts  6.15 us (6%)
  other arithmetic  1.88 us (2%)
    pallas_call x1, Pallas kernels, attend_exchange(): pl.pallas_call(functools.partial(attend_kernel, n, scale), out_shape=jax....  38.7 us
    pallas_call x2, Pallas kernels, pair_sum_exchange(): pl.pallas_call(functools.partial(pair_sum_kernel, half, final), out_shape...  23.1 us
    pallas_call x1, Pallas kernels, dispatch(): pl.pallas_call(functools.partial(dispatch_kernel, half, share), out_shape...  11.4 us
    dot_general x1, matrix products, shards(): jnp.dot(v_flat, w_out, preferred_element_type=jnp.float32)  7.93 us
    dot_general x1, matrix products, shards(): jnp.dot(act, w_down, preferred_element_type=jnp.float32)  7.88 us
    dot_general x1, matrix products, shards(): gate = jnp.dot(stacked, w_gate, preferred_element_type=jnp.float32)  4.42 us

profile of v4, /device:TPU:0, one launch (start us, length us, event | category | flops | bytes accessed | tf_op | source)
XLA Modules:
  0.0 105.8 jit_solution(10392406840600929008)
XLA Ops:
  0.6 0.0 copy-start
  0.6 1.0 slice.7
  1.7 0.9 slice.6
  2.6 0.0 copy-done
  2.6 0.3 fusion.1
  2.9 0.1 pad_maximum_fusion
  3.0 0.4 copy.37
  3.4 1.5 %copy.38.cache_ref = bf16[2,384,576]{2,1,0:T(8,128)(2,1)S(1)} copy(bf16[2,384,576]{1,2,0:T(8,128)(2,1)} %param.17) | data formatting | bytes 1769472 | tf_op args[3]
  4.9 0.7 reshape.166
  5.6 0.7 compare_convert_fusion.keep_ref
  6.4 38.7 %shard_map.149 = bf16[16,32,512]{2,1,0:T(8,128)(2,1)S(1)} custom-call(bf16[16,32,576]{2,1,0:T(8,128)(2,1)S(1)} %bitcast.29, bf16[2,384,576]{2,1,0:T(8,128)(2,1)S(1)} %copy.38.cache_ref, bf16[2,16,576]{2,1,0:T(8,128)(2,1)S(1)} %pad.4.fresh_ref, f32[2,1,384]{2,1,0:T(1,128)S(1)} %compare_convert_fusion.keep_ref), custom_call_target="tpu_custom_call" | custom-call | tf_op jit(solution)/shard_map/pallas_call | solution.py:222
  45.1 1.6 %fusion.2 = bf16[8,8,8,128]{3,2,1,0:T(8,128)(2,1)S(1)} fusion(bf16[8,512,128]{2,1,0:T(8,128)(2,1)} %param.20, bf16[64,8,512]{2,1,0:T(8,128)(2,1)S(1)} %bitcast.30), kind=kOutput, calls=%fused_computation.8 | convolution fusion | flops 67174400 | bytes 1703936 | tf_op jit(solution)/shard_map/thc,hcv->thv/dot_general | solution.py:468
  46.7 0.0 copy-start.1
  46.7 0.0 copy-start.3
  46.7 0.0 copy-start.4
  46.7 0.0 copy-start.2
  46.8 7.9 %convolution_convert_fusion = bf16[64,7168]{1,0:T(8,128)(2,1)S(1)} fusion(bf16[1024,7168]{1,0:T(8,128)(2,1)} %param.21, bf16[8,8,8,128]{3,2,1,0:T(8,128)(2,1)S(1)} %fusion.2), kind=kOutput, calls=%fused_computation | convolution fusion | flops 939982848 | bytes 15728640 | tf_op jit(solution)/shard_map/dot_general | solution.py:472
  54.7 0.4 reshape.169.in_ref
  55.1 12.2 %shard_map.150 = f32[32,896]{1,0:T(8,128)S(1)} custom-call(bf16[16,32,896]{2,1,0:T(8,128)(2,1)S(1)} %reshape.169.in_ref), custom_call_target="tpu_custom_call" | custom-call | tf_op jit(solution)/shard_map/pallas_call | solution.py:341
  67.4 0.0 copy-done.1
  67.4 0.8 multiply_reduce_fusion
  68.2 0.0 copy-done.3
  68.2 0.1 copy.42
  68.3 0.1 broadcast_in_dim.10
  68.3 0.0 copy-done.4
  68.3 0.1 copy.41
  68.4 0.1 eq.73
  68.5 0.1 iota_compare_fusion.1
  68.6 0.2 select_reduce_fusion
  68.8 0.1 fusion.18
  69.0 0.2 convolution_convert_fusion.5
  69.2 0.1 copy.43
  69.3 0.0 copy-done.2
  69.3 0.3 convolution_convert_fusion.2
  69.6 0.1 reshape.172.in_ref
  69.7 11.4 %shard_map.151 = bf16[16,16,896]{2,1,0:T(8,128)(2,1)S(1)} custom-call(bf16[8,16,896]{2,1,0:T(8,128)(2,1)S(1)} %reshape.172.in_ref), custom_call_target="tpu_custom_call" | custom-call | tf_op jit(solution)/shard_map/pallas_call | solution.py:411
  81.1 0.2 reshape.173
  81.3 4.4 %fusion.33 = f32[32,512]{1,0:T(8,128)S(1)} fusion(bf16[32,7168]{1,0:T(8,128)(2,1)S(1)} %reshape.173, bf16[7168,512]{1,0:T(8,128)(2,1)} %param.23), kind=kOutput, calls=%fused_computation.55 | convolution fusion | flops 234881024 | bytes 7864320 | tf_op jit(solution)/shard_map/dot_general | solution.py:497
  85.7 7.9 %convolution_convert_fusion.1 = bf16[32,7168]{1,0:T(8,128)(2,1)S(1)} fusion(bf16[512,7168]{1,0:T(8,128)(2,1)} %param.25, bf16[32,7168]{1,0:T(8,128)(2,1)S(1)} %reshape.173, bf16[7168,512]{1,0:T(8,128)(2,1)} %param.24, f32[32,512]{1,0:T(8,128)S(1)} %fusion.33), kind=kOutput, calls=%fused_computation.1 | convolution fusion | flops 470089728 | bytes 15663104 | tf_op jit(solution)/shard_map/dot_general | solution.py:500
  93.6 0.2 reshape.174.in_ref
  93.8 10.9 %shard_map.152 = bf16[8,16,896]{2,1,0:T(8,128)(2,1)S(1)} custom-call(bf16[16,16,896]{2,1,0:T(8,128)(2,1)S(1)} %reshape.174.in_ref), custom_call_target="tpu_custom_call" | custom-call | tf_op jit(solution)/shard_map/pallas_call | solution.py:341
  104.8 0.1 reduce_sum.26
  104.8 0.9 fusion
  (7 shorter events, 0.1 us)
Async XLA Ops:
  0.6 2.0 %copy-start = (bf16[8,128,512]{2,1,0:T(8,128)(2,1)S(1)}, bf16[8,128,512]{2,1,0:T(8,128)(2,1)}, u32[]{:S(2)}) copy-start(bf16[8,128,512]{2,1,0:T(8,128)(2,1)} %param.19) | copy-start | bytes 3145732
  46.7 20.7 %copy-start.1 = (bf16[4,7168]{1,0:T(4,128)(2,1)S(1)}, bf16[4,7168]{1,0:T(4,128)(2,1)}, u32[]{:S(2)}) copy-start(bf16[4,7168]{1,0:T(4,128)(2,1)} %param.14) | copy-start | bytes 172036
  46.7 21.4 %copy-start.3 = (f32[4,2]{0,1:T(2,128)S(1)}, f32[4,2]{0,1:T(2,128)}, u32[]{:S(2)}) copy-start(f32[4,2]{0,1:T(2,128)} %param.27) | copy-start | bytes 100
  46.7 21.6 %copy-start.4 = (s32[4,2]{0,1:T(2,128)S(1)}, s32[4,2]{0,1:T(2,128)}, u32[]{:S(2)}) copy-start(s32[4,2]{0,1:T(2,128)} %param.26) | copy-start | bytes 100
  46.7 22.5 %copy-start.2 = (f32[7168]{0:T(1024)S(1)}, f32[7168]{0:T(1024)}, u32[]{:S(2)}) copy-start(f32[7168]{0:T(1024)} %param.22) | copy-start | bytes 86020
